TPU v7x, 32 devices: a whole 2x2x4 slice. The times are simulated.
32 devices in a mesh: frame: 8 (over y, x, core), head: 4 (over z).
Axes of the slice: x: 2, y: 2, z: 4, core: 2. Of those that a mesh axis runs over, the one named last changes fastest.
Arguments:
- queries: bfloat16 [8192, 5120], P(('frame', 'head'))
- keys: bfloat16 [8192, 5120], P(('frame', 'head'))
- values: bfloat16 [8192, 5120], P(('frame', 'head')), may hold values from -6 to 6
- out_grad: bfloat16 [8192, 5120], P(('frame', 'head')), may hold values from -6 to 6
- memory_frames: int32 [8, 7], replicated, may hold values from 0 to 127, as said below
- frame_tokens: int32 [128], replicated, may hold values from 32 to 64
Outputs:
- attn_out: bfloat16 [8192, 5120], P(('frame', 'head'))
- query_grad: bfloat16 [8192, 5120], P(('frame', 'head'))
- key_grad: bfloat16 [8192, 5120], P(('frame', 'head'))
- value_grad: bfloat16 [8192, 5120], P(('frame', 'head'))
Inputs may be any that keep to these rules, and one draw needn't show every extreme that they name: `memory_frames`: entry i of row c names a frame of group (c - 1 - i) mod 8.
All inputs are finite; a program needn't handle non-finite values.
Results may differ from a plain program's by a relative error of at most 0.0069.
Values may be sent and summed in bfloat16 or wider, within the bound.
A program may use at most 320 MiB of HBM per device.

v0:
```python
from functools import reduce
import math

import jax
import jax.numpy as jnp
from jax import lax
from jax.sharding import PartitionSpec as P

HEAD_DIM = 128
TF = 64
FRAMES_DEV = 16


def attend(query_rows, grad_rows, blocks, score_scale):
    scores = []
    for member in blocks:
        unmasked = (
            jnp.einsum("rd,kd->rk", query_rows, member[0], preferred_element_type=jnp.float32)
            * score_scale
        )
        scores.append(jnp.where(member[2][None, :], unmasked, -jnp.inf))
    row_top = reduce(jnp.maximum, [jnp.max(entry, axis=1) for entry in scores])
    powers = [jnp.exp(entry - row_top[:, None]) for entry in scores]
    row_total = reduce(jnp.add, [jnp.sum(entry, axis=1) for entry in powers])
    weights = [entry / row_total[:, None] for entry in powers]
    rounded = [entry.astype(jnp.bfloat16) for entry in weights]
    out_sum = reduce(
        jnp.add,
        [
            jnp.dot(weight, member[1], preferred_element_type=jnp.float32)
            for weight, member in zip(rounded, blocks)
        ],
    )
    weight_grads = [
        jnp.einsum("rd,kd->rk", grad_rows, member[1], preferred_element_type=jnp.float32)
        for member in blocks
    ]
    row_delta = reduce(
        jnp.add, [jnp.sum(weight * grads, axis=1) for weight, grads in zip(weights, weight_grads)]
    )
    score_grads = [
        (weight * (grads - row_delta[:, None])).astype(jnp.bfloat16)
        for weight, grads in zip(weights, weight_grads)
    ]
    query_sum = reduce(
        jnp.add,
        [
            jnp.dot(grads, member[0], preferred_element_type=jnp.float32)
            for grads, member in zip(score_grads, blocks)
        ],
    )
    key_parts = [
        jnp.einsum("rk,rd->kd", grads, query_rows, preferred_element_type=jnp.float32) * score_scale
        for grads in score_grads
    ]
    value_parts = [
        jnp.einsum("rk,rd->kd", weight, grad_rows, preferred_element_type=jnp.float32)
        for weight in rounded
    ]
    return (
        out_sum.astype(jnp.bfloat16),
        (query_sum * score_scale).astype(jnp.bfloat16),
        key_parts[0],
        value_parts[0],
    )


def local(queries, keys, values, out_grad, memory_frames, frame_tokens):
    queries_here, keys_here, values_here, grads_here = (
        lax.all_to_all(queries, "head", split_axis=1, concat_axis=0, tiled=True),
        lax.all_to_all(keys, "head", split_axis=1, concat_axis=0, tiled=True),
        lax.all_to_all(values, "head", split_axis=1, concat_axis=0, tiled=True),
        lax.all_to_all(out_grad, "head", split_axis=1, concat_axis=0, tiled=True),
    )
    row_count, feat_width = queries_here.shape
    groups = lax.axis_size("frame")
    frame_index = lax.axis_index("frame")
    score_scale = 1.0 / math.sqrt(HEAD_DIM)
    token_pos = jnp.arange(TF, dtype=jnp.int32)
    frame_range = jnp.arange(FRAMES_DEV, dtype=jnp.int32)
    all_frames = jnp.arange(frame_tokens.shape[0], dtype=jnp.int32)
    own_counts = lax.dynamic_slice_in_dim(frame_tokens, frame_index * FRAMES_DEV, FRAMES_DEV)
    own_live = (token_pos[None, :] < own_counts[:, None]).reshape(row_count)
    my_frames = lax.dynamic_index_in_dim(memory_frames, frame_index, 0, keepdims=False)
    my_owners = my_frames // FRAMES_DEV
    mem_slots = my_frames.shape[0]
    owner_table = memory_frames // FRAMES_DEV
    local_table = memory_frames % FRAMES_DEV
    asked_me = owner_table == frame_index
    picked = jnp.sum(jnp.where(asked_me, local_table, 0), axis=1)
    wanted = jnp.any(asked_me, axis=1)
    selector = ((picked[:, None] == frame_range[None, :]) & wanted[:, None]).astype(jnp.bfloat16)
    key_send = jnp.dot(
        selector, keys_here.reshape(FRAMES_DEV, TF * feat_width), preferred_element_type=jnp.float32
    )
    value_send = jnp.dot(
        selector,
        values_here.reshape(FRAMES_DEV, TF * feat_width),
        preferred_element_type=jnp.float32,
    )
    key_send = key_send.astype(jnp.bfloat16).reshape(groups, TF, feat_width)
    value_send = value_send.astype(jnp.bfloat16).reshape(groups, TF, feat_width)
    fetched_keys, fetched_values = (
        lax.all_to_all(key_send, "frame", split_axis=0, concat_axis=0, tiled=True),
        lax.all_to_all(value_send, "frame", split_axis=0, concat_axis=0, tiled=True),
    )
    mem_keys = jnp.take(fetched_keys, my_owners, axis=0).reshape(mem_slots * TF, feat_width)
    mem_values = jnp.take(fetched_values, my_owners, axis=0).reshape(mem_slots * TF, feat_width)
    mem_counts = jnp.sum(
        jnp.where(my_frames[:, None] == all_frames[None, :], frame_tokens[None, :], 0), axis=1
    )
    mem_live = (token_pos[None, :] < mem_counts[:, None]).reshape(mem_slots * TF)
    key_sets = (
        (
            jnp.concatenate([keys_here, mem_keys], 0),
            jnp.concatenate([values_here, mem_values], 0),
            jnp.concatenate([own_live, mem_live], 0),
        ),
    )
    out_cols, query_cols, key_cols, value_cols = ([], [], [], [])
    for head_num in range(feat_width // HEAD_DIM):
        first_col = head_num * HEAD_DIM
        last_col = first_col + HEAD_DIM
        blocks = [
            (member[0][:, first_col:last_col], member[1][:, first_col:last_col], member[2])
            for member in key_sets
        ]
        head_out, head_qg, head_kg, head_vg = attend(
            queries_here[:, first_col:last_col],
            grads_here[:, first_col:last_col],
            blocks,
            score_scale,
        )
        out_cols.append(head_out)
        query_cols.append(head_qg)
        key_cols.append(head_kg)
        value_cols.append(head_vg)
    attn_out = jnp.concatenate(out_cols, 1)
    query_grad = jnp.concatenate(query_cols, 1)
    key_total = jnp.concatenate(key_cols, 1)
    value_total = jnp.concatenate(value_cols, 1)
    mem_kg = key_total[row_count:].astype(jnp.bfloat16).reshape(mem_slots, TF, feat_width)
    mem_vg = value_total[row_count:].astype(jnp.bfloat16).reshape(mem_slots, TF, feat_width)
    back_keys = jnp.zeros((groups, TF, feat_width), jnp.bfloat16).at[my_owners].set(mem_kg)
    back_values = jnp.zeros((groups, TF, feat_width), jnp.bfloat16).at[my_owners].set(mem_vg)
    summed_keys = jnp.einsum(
        "rf,rtc->ftc",
        selector,
        lax.all_to_all(back_keys, "frame", split_axis=0, concat_axis=0, tiled=True),
        preferred_element_type=jnp.float32,
    )
    summed_values = jnp.einsum(
        "rf,rtc->ftc",
        selector,
        lax.all_to_all(back_values, "frame", split_axis=0, concat_axis=0, tiled=True),
        preferred_element_type=jnp.float32,
    )
    key_grad = (key_total[:row_count] + summed_keys.reshape(row_count, feat_width)).astype(
        jnp.bfloat16
    )
    value_grad = (value_total[:row_count] + summed_values.reshape(row_count, feat_width)).astype(
        jnp.bfloat16
    )
    return (
        lax.all_to_all(attn_out, "head", split_axis=0, concat_axis=1, tiled=True),
        lax.all_to_all(query_grad, "head", split_axis=0, concat_axis=1, tiled=True),
        lax.all_to_all(key_grad, "head", split_axis=0, concat_axis=1, tiled=True),
        lax.all_to_all(value_grad, "head", split_axis=0, concat_axis=1, tiled=True),
    )


def solution(mesh):
    placed = (
        P(("frame", "head"), None),
        P(("frame", "head"), None),
        P(("frame", "head"), None),
        P(("frame", "head"), None),
        P(),
        P(),
    )
    return jax.shard_map(
        local,
        mesh=mesh,
        in_specs=placed,
        out_specs=(
            P(("frame", "head"), None),
            P(("frame", "head"), None),
            P(("frame", "head"), None),
            P(("frame", "head"), None),
        ),
        check_vma=False,
    )
```

profile of v0, /device:TPU:0, one launch (start us, length us, event | category | flops | bytes accessed | tf_op | source)
XLA Modules:
  0.0 894.0 jit_solution(4036383417655957820)
XLA Ops:
  5.0 6.3 all-to-all-start.3
  15.7 55.1 %all-to-all-done.3 = bf16[256,4,1280]{0,2,1:T(8,128)(2,1)S(1)} async-done(((bf16[256,4,1280]{0,2,1:T(8,128)(2,1)}), bf16[256,4,1280]{0,2,1:T(8,128)(2,1)S(1)}, u32[]{:S(2)}, u32[]{:S(2)}) %all-to-all-start.3) | async-done | bytes 2621472 | tf_op jit(solution)/shard_map/all_to_all | solution.py:72
  70.8 4.5 all-to-all-start
  79.7 54.6 %all-to-all-done = bf16[256,4,1280]{0,2,1:T(8,128)(2,1)} async-done(((bf16[256,4,1280]{0,2,1:T(8,128)(2,1)}), bf16[256,4,1280]{0,2,1:T(8,128)(2,1)}, u32[]{:S(2)}, u32[]{:S(2)}) %all-to-all-start) | async-done | bytes 2621472 | tf_op jit(solution)/shard_map/all_to_all | solution.py:71
  142.4 54.5 %all-to-all-done.2 = bf16[256,4,1280]{0,2,1:T(8,128)(2,1)S(1)} async-done(((bf16[256,4,1280]{0,2,1:T(8,128)(2,1)}), bf16[256,4,1280]{0,2,1:T(8,128)(2,1)S(1)}, u32[]{:S(2)}, u32[]{:S(2)}) %all-to-all-start.2) | async-done | bytes 2621472 | tf_op jit(solution)/shard_map/all_to_all | solution.py:70
  196.9 4.5 all-to-all-start.6
  210.7 49.7 %all-to-all-done.6 = bf16[256,4,1280]{0,2,1:T(8,128)(2,1)} async-done(((bf16[256,4,1280]{0,2,1:T(8,128)(2,1)}), bf16[256,4,1280]{0,2,1:T(8,128)(2,1)}, u32[]{:S(2)}, u32[]{:S(2)}) %all-to-all-start.6) | async-done | bytes 2621472 | tf_op jit(solution)/shard_map/all_to_all | solution.py:73
  276.2 6.7 all-to-all-done.1
  292.7 4.6 copy.81
  300.3 5.1 all-to-all-done.4
  366.1 25.4 %fusion.60 = (f32[1024]{0:T(1024)S(1)}, f32[1024]{0:T(1024)S(1)}, f32[1024]{0:T(1024)S(1)}, f32[1024]{0:T(1024)S(1)}, f32[1024]{0:T(1024)S(1)}, /*index=5*/f32[1...) fusion(f32[1472,1024]{1,0:T(8,128)} %get-tuple-element.60, ...), kind=kOutput, calls=%fused_computation.154 | convolution fusion | flops 434853888 | bytes 64374208 | tf_op jit(solution)/shard_map/rd,kd->rk/dot_general | solution.py:18
  391.5 4.6 fusion.125
  400.1 18.2 %fusion.58 = (f32[1024]{0:T(1024)S(1)}, f32[1024]{0:T(1024)S(1)}, f32[1024]{0:T(1024)S(1)}, f32[1024]{0:T(1024)S(1)}, f32[1024]{0:T(1024)S(1)}, /*index=5*/f32[1024]{0:T(1024)S(1)}, f32[1024]{0:T(1024)S(1)}, f32[1024]{0:T(1024)S(1)}) fusion(f32[1472,1024]{1,0:T(8,128)} %fusion.178, f32[1024]{0:T(1024)S(1)} %get-tuple-element.31, ...), kind=kLoop, calls=%fused_computation.152 | loop fusion | flops 48226304 | bytes 48301504 | tf_op jit(solution)/shard_map/reduce_sum | solution.py:24
  430.7 18.9 %fusion = (f32[1024]{0:T(1024)S(1)}, f32[1024]{0:T(1024)S(1)}, f32[1024]{0:T(1024)S(1)}, f32[1024]{0:T(1024)S(1)}, f32[1472,1024]{1,0:T(8,128)}) fusion(f32[1024]{0:T(1024)S(1)} %get-tuple-element.23, f32[1024]{0:T(1024)S(1)} %get-tuple-element.33, f32[1472,1024]{1,0:T(8,128)} %get-tuple-element.60, pred[1472]{0:T(1024)(128)(4,1)S(1)} %pad_add_fusion, ...), kind=kOutput, calls=%fused_computation.26 | convolution fusion | flops 422047744 | bytes 48924096 | tf_op jit(solution)/shard_map/rd,kd->rk/dot_general | solution.py:35
  449.6 16.6 %fusion.6 = (f32[1024]{0:T(1024)S(1)}, f32[1024]{0:T(1024)S(1)}, bf16[1024,1472]{0,1:T(8,128)(2,1)}, f32[1472,1024]{1,0:T(8,128)}) fusion(f32[1024]{0:T(1024)S(1)} %get-tuple-element.42, f32[1024]{0:T(1024)S(1)} %get-tuple-element.30, f32[1472,1024]{1,0:T(8,128)} %fusion.181, pred[1472]{0:T(1024)(128)(4,1)S(1)} %pad_add_fusion, f32[1472,1024]{1,0:T(8,128)} %fusion.154, ...), kind=kOutput, calls=%fused_computation.36 | convolution fusion | flops 415266816 | bytes 43259328 | tf_op jit(solution)/shard_map/rd,kd->rk/dot_general | solution.py:35
  466.2 18.8 %fusion.3 = (f32[1024]{0:T(1024)S(1)}, f32[1024]{0:T(1024)S(1)}, f32[1024]{0:T(1024)S(1)}, f32[1024]{0:T(1024)S(1)}, f32[1472,1024]{1,0:T(8,128)}) fusion(f32[1024]{0:T(1024)S(1)} %get-tuple-element.35, f32[1024]{0:T(1024)S(1)} %get-tuple-element.31, f32[1472,1024]{1,0:T(8,128)} %fusion.178, pred[1472]{0:T(1024)(128)(4,1)S(1)} %pad_add_fusion, ...), kind=kOutput, calls=%fused_computation.31 | convolution fusion | flops 422801408 | bytes 52315584 | tf_op jit(solution)/shard_map/rd,kd->rk/dot_general | solution.py:35
  485.0 16.3 %fusion.11 = (bf16[1024,1472]{0,1:T(8,128)(2,1)}, bf16[1024,1472]{0,1:T(8,128)(2,1)S(1)}, bf16[1024,1472]{0,1:T(8,128)(2,1)}) fusion(f32[1472,1024]{1,0:T(8,128)} %fusion.154, f32[1024]{0:T(1024)S(1)} %get-tuple-element.22, f32[1024]{0:T(1024)S(1)} %get-tuple-element.41, f32[1024]{0:T(1024)S(1)} %get-tuple-element.29, f32[1472,1024]{1,0:T(8,128)} %fusion.184, ...), kind=kLoop, calls=%fused_computation.43 | loop fusion | flops 31653888 | bytes 45258176 | tf_op jit(solution)/shard_map/convert_element_type | solution.py:42
  505.9 19.1 %fusion.8 = (bf16[1024,1472]{0,1:T(8,128)(2,1)}, bf16[1024,1472]{0,1:T(8,128)(2,1)}, bf16[1024,1472]{0,1:T(8,128)(2,1)}) fusion(f32[1472,1024]{1,0:T(8,128)} %get-tuple-element.63, f32[1024]{0:T(1024)S(1)} %get-tuple-element.21, f32[1024]{0:T(1024)S(1)} %get-tuple-element.42, f32[1024]{0:T(1024)S(1)} %get-tuple-element.30, f32[1472,1024]{1,0:T(8,128)} %fusion.181, ...), kind=kLoop, calls=%fused_computation.38 | loop fusion | flops 31653888 | bytes 45258176 | tf_op jit(solution)/shard_map/convert_element_type | solution.py:42
  531.8 13.7 %fusion.2 = (bf16[1024,1472]{0,1:T(8,128)(2,1)}, bf16[1024,1472]{0,1:T(8,128)(2,1)}, bf16[1024,1472]{0,1:T(8,128)(2,1)}) fusion(f32[1472,1024]{1,0:T(8,128)} %get-tuple-element.62, f32[1024]{0:T(1024)S(1)} %get-tuple-element.13, f32[1024]{0:T(1024)S(1)} %get-tuple-element.23, f32[1024]{0:T(1024)S(1)} %get-tuple-element.33, f32[1472,1024]{1,0:T(8,128)S(1)} %bitcast.382, ...), kind=kLoop, calls=%fused_computation.28 | loop fusion | flops 31653888 | bytes 45258176 | tf_op jit(solution)/shard_map/convert_element_type | solution.py:42
  572.5 5.5 convolution_dynamic-update-slice_fusion.8
  578.1 5.4 convolution_dynamic-update-slice_fusion.7
  611.1 5.1 fusion.111
  620.5 5.2 fusion.109
  625.7 4.8 fusion.107
  634.0 4.7 all-to-all-done.10
  638.7 4.6 all-to-all-start.5
  657.0 43.1 %all-to-all-done.5 = bf16[4,256,1280]{1,2,0:T(8,128)(2,1)} async-done(((bf16[4,256,1280]{1,2,0:T(8,128)(2,1)}), bf16[4,256,1280]{1,2,0:T(8,128)(2,1)}, u32[]{:S(2)}, u32[]{:S(2)}) %all-to-all-start.5) | async-done | bytes 2621472 | tf_op jit(solution)/shard_map/all_to_all | solution.py:165
  711.9 51.0 %all-to-all-done.7 = bf16[4,256,1280]{1,2,0:T(8,128)(2,1)S(1)} async-done(((bf16[4,256,1280]{1,2,0:T(8,128)(2,1)}), bf16[4,256,1280]{1,2,0:T(8,128)(2,1)S(1)}, u32[]{:S(2)}, u32[]{:S(2)}) %all-to-all-start.7) | async-done | bytes 2621472 | tf_op jit(solution)/shard_map/all_to_all | solution.py:166
  762.9 4.6 all-to-all-start.9
  775.3 51.1 %all-to-all-done.9 = bf16[4,256,1280]{2,1,0:T(8,128)(2,1)} async-done(((bf16[4,256,1280]{2,1,0:T(8,128)(2,1)}), bf16[4,256,1280]{2,1,0:T(8,128)(2,1)}, u32[]{:S(2)}, u32[]{:S(2)}) %all-to-all-start.9) | async-done | bytes 2621472 | tf_op jit(solution)/shard_map/all_to_all | solution.py:167
  826.5 4.5 all-to-all-start.11
  841.7 48.3 %all-to-all-done.11 = bf16[4,256,1280]{2,1,0:T(8,128)(2,1)} async-done(((bf16[4,256,1280]{2,1,0:T(8,128)(2,1)}), bf16[4,256,1280]{2,1,0:T(8,128)(2,1)}, u32[]{:S(2)}, u32[]{:S(2)}) %all-to-all-start.11) | async-done | bytes 2621472 | tf_op jit(solution)/shard_map/all_to_all | solution.py:168
  (282 shorter events, 256.8 us)
Async XLA Ops:
  5.0 65.8 %all-to-all-start.3 = ((bf16[256,4,1280]{0,2,1:T(8,128)(2,1)}), bf16[256,4,1280]{0,2,1:T(8,128)(2,1)S(1)}, u32[]{:S(2)}, u32[]{:S(2)}) async-start(bf16[256,4,1280]{0,2,1:T(8,128)(2,1)} %bitcast.413), calls=%async_computation.3 | async-start | bytes 5242880 | tf_op jit(solution)/shard_map/all_to_all | solution.py:72
  70.8 63.6 %copy-start.31 = (bf16[256,4,1280]{0,2,1:T(8,128)(2,1)}, bf16[256,4,1280]{0,2,1:T(8,128)(2,1)S(1)}, u32[]{:S(2)}) copy-start(bf16[256,4,1280]{0,2,1:T(8,128)(2,1)S(1)} %all-to-all-done.3) | copy-start | bytes 7864324
  70.8 63.5 %all-to-all-start = ((bf16[256,4,1280]{0,2,1:T(8,128)(2,1)}), bf16[256,4,1280]{0,2,1:T(8,128)(2,1)}, u32[]{:S(2)}, u32[]{:S(2)}) async-start(bf16[256,4,1280]{0,2,1:T(8,128)(2,1)} %bitcast.411), calls=%async_computation | async-start | bytes 5242880 | tf_op jit(solution)/shard_map/all_to_all | solution.py:71
  134.3 62.5 %all-to-all-start.2 = ((bf16[256,4,1280]{0,2,1:T(8,128)(2,1)}), bf16[256,4,1280]{0,2,1:T(8,128)(2,1)S(1)}, u32[]{:S(2)}, u32[]{:S(2)}) async-start(bf16[256,4,1280]{0,2,1:T(8,128)(2,1)} %bitcast.412), calls=%async_computation.2 | async-start | bytes 5242880 | tf_op jit(solution)/shard_map/all_to_all | solution.py:70
  138.0 63.5 %copy-start.39 = (s32[8,7]{1,0:T(8,128)S(1)}, s32[8,7]{1,0:T(8,128)}, u32[]{:S(2)}) copy-start(s32[8,7]{1,0:T(8,128)} %param.12) | copy-start | bytes 676
  196.9 63.5 %all-to-all-start.6 = ((bf16[256,4,1280]{0,2,1:T(8,128)(2,1)}), bf16[256,4,1280]{0,2,1:T(8,128)(2,1)}, u32[]{:S(2)}, u32[]{:S(2)}) async-start(bf16[256,4,1280]{0,2,1:T(8,128)(2,1)} %bitcast.409), calls=%async_computation.6 | async-start | bytes 5242880 | tf_op jit(solution)/shard_map/all_to_all | solution.py:73
  201.6 71.1 %copy-start.40 = (pred[8]{0:T(512)(128)(4,1)}, pred[8]{0:T(512)(128)(4,1)S(1)}, u32[]{:S(2)}) copy-start(pred[8]{0:T(512)(128)(4,1)S(1)} %get-tuple-element.46) | copy-start | bytes 28
  201.7 71.0 %copy-start.42 = (s32[8]{0:T(128)}, s32[8]{0:T(128)S(1)}, u32[]{:S(2)}) copy-start(s32[8]{0:T(128)S(1)} %fusion.206) | copy-start | bytes 100
  204.7 161.4 %copy-start = (bf16[4,256,1280]{2,1,0:T(8,128)(2,1)}, bf16[4,256,1280]{2,1,0:T(8,128)(2,1)S(1)}, u32[]{:S(2)}) copy-start(bf16[4,256,1280]{2,1,0:T(8,128)(2,1)S(1)} %copy.70) | copy-start | bytes 7864324
  260.4 22.5 %all-to-all-start.1 = ((bf16[8,64,1280]{2,1,0:T(8,128)(2,1)}), bf16[8,64,1280]{2,1,0:T(8,128)(2,1)}, u32[]{:S(2)}, u32[]{:S(2)}) async-start(bf16[8,64,1280]{2,1,0:T(8,128)(2,1)} %copy.72), calls=%async_computation.1 | async-start | bytes 2621440 | tf_op jit(solution)/shard_map/all_to_all | solution.py:104
  282.9 22.5 %all-to-all-start.4 = ((bf16[8,64,1280]{2,1,0:T(8,128)(2,1)}), bf16[8,64,1280]{2,1,0:T(8,128)(2,1)}, u32[]{:S(2)}, u32[]{:S(2)}) async-start(bf16[8,64,1280]{2,1,0:T(8,128)(2,1)} %copy.78), calls=%async_computation.4 | async-start | bytes 2621440 | tf_op jit(solution)/shard_map/all_to_all | solution.py:105
  310.4 22.8 %copy-start.2 = (bf16[7,64,1280]{2,1,0:T(8,128)(2,1)}, bf16[7,64,1280]{2,1,0:T(8,128)(2,1)S(1)}, u32[]{:S(2)}) copy-start(bf16[7,64,1280]{2,1,0:T(8,128)(2,1)S(1)} %get-tuple-element.58) | copy-start | bytes 3440644
  310.4 48.8 %copy-start.8 = (bf16[7,64,1280]{2,1,0:T(8,128)(2,1)}, bf16[7,64,1280]{2,1,0:T(8,128)(2,1)S(1)}, u32[]{:S(2)}) copy-start(bf16[7,64,1280]{2,1,0:T(8,128)(2,1)S(1)} %get-tuple-element.59) | copy-start | bytes 3440644
  310.5 52.2 %copy-start.35 = (bf16[1472,128]{1,0:T(8,128)(2,1)}, bf16[1472,128]{1,0:T(8,128)(2,1)S(1)}, u32[]{:S(2)}) copy-start(bf16[1472,128]{1,0:T(8,128)(2,1)S(1)} %pad_maximum_fusion.1) | copy-start | bytes 1130500
  311.8 50.9 %copy-start.6 = (f32[1472,1024]{1,0:T(8,128)}, f32[1472,1024]{1,0:T(8,128)S(1)}, u32[]{:S(2)}) copy-start(f32[1472,1024]{1,0:T(8,128)S(1)} %fusion.202) | copy-start | bytes 18087940
  400.1 18.2 %copy-start.5 = (bf16[4,256,1280]{2,1,0:T(8,128)(2,1)S(1)}, bf16[4,256,1280]{2,1,0:T(8,128)(2,1)}, u32[]{:S(2)}) copy-start(bf16[4,256,1280]{2,1,0:T(8,128)(2,1)} %copy.76) | copy-start | bytes 7864324
  400.1 18.2 %copy-start.9 = (bf16[7,64,1280]{2,1,0:T(8,128)(2,1)S(1)}, bf16[7,64,1280]{2,1,0:T(8,128)(2,1)}, u32[]{:S(2)}) copy-start(bf16[7,64,1280]{2,1,0:T(8,128)(2,1)} %copy-done.8) | copy-start | bytes 3440644
  400.1 20.0 %slice-start.24 = ((s8[6029312]{0:T(1024)(128)(4,1)}), s8[4194304]{0:T(1024)(128)(4,1)S(1)}, s32[]{:S(2)}) async-start(s8[6029312]{0:T(1024)(128)(4,1)} %bitcast.379), calls=%async_computation.36 | async-start | bytes 8388608
  503.0 28.8 %slice-start = ((s8[6029312]{0:T(1024)(128)(4,1)}), s8[4194304]{0:T(1024)(128)(4,1)S(1)}, s32[]{:S(2)}) async-start(s8[6029312]{0:T(1024)(128)(4,1)} %bitcast.336), calls=%async_computation.12 | async-start | bytes 8388608
  503.0 28.8 %slice-start.20 = ((s8[6029312]{0:T(1024)(128)(4,1)}), s8[4194304]{0:T(1024)(128)(4,1)S(1)}, s32[]{:S(2)}) async-start(s8[6029312]{0:T(1024)(128)(4,1)} %bitcast.356), calls=%async_computation.32 | async-start | bytes 8388608
  503.0 28.8 %slice-start.26 = ((s8[6029312]{0:T(1024)(128)(4,1)}), s8[4194304]{0:T(1024)(128)(4,1)S(1)}, s32[]{:S(2)}) async-start(s8[6029312]{0:T(1024)(128)(4,1)} %bitcast.381), calls=%async_computation.38 | async-start | bytes 8388608
  505.9 25.8 %slice-start.1 = ((s8[6029312]{0:T(1024)(128)(4,1)}), s8[1835008]{0:T(1024)(128)(4,1)S(1)}, s32[]{:S(2)}) async-start(s8[6029312]{0:T(1024)(128)(4,1)} %bitcast.336), calls=%async_computation.13 | async-start | bytes 3670016
  505.9 25.9 %slice-start.21 = ((s8[6029312]{0:T(1024)(128)(4,1)}), s8[1835008]{0:T(1024)(128)(4,1)S(1)}, s32[]{:S(2)}) async-start(s8[6029312]{0:T(1024)(128)(4,1)} %bitcast.356), calls=%async_computation.33 | async-start | bytes 3670016
  505.9 25.9 %slice-start.27 = ((s8[6029312]{0:T(1024)(128)(4,1)}), s8[1835008]{0:T(1024)(128)(4,1)S(1)}, s32[]{:S(2)}) async-start(s8[6029312]{0:T(1024)(128)(4,1)} %bitcast.381), calls=%async_computation.39 | async-start | bytes 3670016
  568.1 48.1 %all-to-all-start.8 = ((bf16[8,64,1280]{2,1,0:T(8,128)(2,1)}), bf16[8,64,1280]{2,1,0:T(8,128)(2,1)}, u32[]{:S(2)}, u32[]{:S(2)}) async-start(bf16[8,64,1280]{2,1,0:T(8,128)(2,1)} %scatter_fusion), calls=%async_computation.8 | async-start | bytes 2621440 | tf_op jit(solution)/shard_map/all_to_all | solution.py:149
  616.2 22.5 %all-to-all-start.10 = ((bf16[8,64,1280]{2,1,0:T(8,128)(2,1)}), bf16[8,64,1280]{2,1,0:T(8,128)(2,1)}, u32[]{:S(2)}, u32[]{:S(2)}) async-start(bf16[8,64,1280]{2,1,0:T(8,128)(2,1)} %scatter_fusion.1), calls=%async_computation.10 | async-start | bytes 2621440 | tf_op jit(solution)/shard_map/all_to_all | solution.py:155
  638.7 61.4 %all-to-all-start.5 = ((bf16[4,256,1280]{1,2,0:T(8,128)(2,1)}), bf16[4,256,1280]{1,2,0:T(8,128)(2,1)}, u32[]{:S(2)}, u32[]{:S(2)}) async-start(bf16[4,256,1280]{1,2,0:T(8,128)(2,1)} %bitcast.407), calls=%async_computation.5 | async-start | bytes 5242880 | tf_op jit(solution)/shard_map/all_to_all | solution.py:165
  655.3 48.7 %copy-start.41 = (pred[8]{0:T(512)(128)(4,1)S(1)}, pred[8]{0:T(512)(128)(4,1)}, u32[]{:S(2)}) copy-start(pred[8]{0:T(512)(128)(4,1)} %copy-done.40) | copy-start | bytes 28
  655.4 48.7 %copy-start.43 = (s32[8]{0:T(128)S(1)}, s32[8]{0:T(128)}, u32[]{:S(2)}) copy-start(s32[8]{0:T(128)} %copy-done.42) | copy-start | bytes 100
  700.1 62.8 %all-to-all-start.7 = ((bf16[4,256,1280]{1,2,0:T(8,128)(2,1)}), bf16[4,256,1280]{1,2,0:T(8,128)(2,1)S(1)}, u32[]{:S(2)}, u32[]{:S(2)}) async-start(bf16[4,256,1280]{1,2,0:T(8,128)(2,1)} %bitcast.410), calls=%async_computation.7 | async-start | bytes 5242880 | tf_op jit(solution)/shard_map/all_to_all | solution.py:166
  762.9 63.6 %all-to-all-start.9 = ((bf16[4,256,1280]{2,1,0:T(8,128)(2,1)}), bf16[4,256,1280]{2,1,0:T(8,128)(2,1)}, u32[]{:S(2)}, u32[]{:S(2)}) async-start(bf16[4,256,1280]{2,1,0:T(8,128)(2,1)} %bitcast.414), calls=%async_computation.9 | async-start | bytes 5242880 | tf_op jit(solution)/shard_map/all_to_all | solution.py:167
  826.5 63.5 %all-to-all-start.11 = ((bf16[4,256,1280]{2,1,0:T(8,128)(2,1)}), bf16[4,256,1280]{2,1,0:T(8,128)(2,1)}, u32[]{:S(2)}, u32[]{:S(2)}) async-start(bf16[4,256,1280]{2,1,0:T(8,128)(2,1)} %bitcast.415), calls=%async_computation.11 | async-start | bytes 5242880 | tf_op jit(solution)/shard_map/all_to_all | solution.py:168
  (60 other events, 244.8 us)
where the time goes:
time: 902 us; the launch traced here: 894 us
  waiting for transfers between devices  424 us (47%)
  matrix products  242 us (27%)
  local copies, waits for them, and re-layouts  96.2 us (11%)
  other arithmetic  75.6 us (8%)
  starting transfers between devices  53.9 us (6%)
    dot_general x10, matrix products, attend(): jnp.einsum('rd,kd->rk', grad_rows, member[1], preferred_element_type=jnp....  79.3 us
    all_to_all x1, waiting for transfers between devices, local(): lax.all_to_all(values, 'head', split_axis=1, concat_axis=0, tiled=True)  55.1 us
    dot_general x10, matrix products, attend(): jnp.einsum('rd,kd->rk', query_rows, member[0], preferred_element_type=jnp...  54.9 us
    all_to_all x1, waiting for transfers between devices, local(): lax.all_to_all(keys, 'head', split_axis=1, concat_axis=0, tiled=True)  54.6 us
    all_to_all x1, waiting for transfers between devices, local(): lax.all_to_all(queries, 'head', split_axis=1, concat_axis=0, tiled=True)  54.5 us
    all_to_all x1, waiting for transfers between devices, local(): lax.all_to_all(key_grad, 'head', split_axis=0, concat_axis=1, tiled=True)  51.1 us
    all_to_all x1, waiting for transfers between devices, local(): lax.all_to_all(query_grad, 'head', split_axis=0, concat_axis=1, tiled=True)  51 us
    all_to_all x1, waiting for transfers between devices, local(): lax.all_to_all(out_grad, 'head', split_axis=1, concat_axis=0, tiled=True)  49.7 us
  transfers between devices with their start and end apart: 12, of which 11 were waited for; matrix products, arithmetic and copies ran while one was open for 16% of the time, Pallas kernels for 0%

commit v1 on v0

v1 whole, which is shorter than its diff:
```python
import functools
import math

import jax
import jax.numpy as jnp
from jax import lax
from jax.experimental import pallas as pl
from jax.experimental.pallas import tpu as pltpu
from jax.sharding import PartitionSpec as P

HEAD_DIM = 128
TF = 64
FRAMES_DEV = 16
ROWS = FRAMES_DEV * TF
QBLOCK = 256
AHEAD = 4
MESH = pl.DeviceIdType.MESH


def attention_kernel(
    dims,
    q_in, k_in, v_in, g_in, bias_ref, pick_ref, spread_ref,
    o_out, dq_out, dk_out, dv_out,
    qg, kv, mem_send, mem_grad, back, outs, acc,
    in_send, in_recv, mem_ssem, mem_rsem, back_ssem, back_rsem, out_send, out_recv,
):
    groups, zs, heads, slots, part, key_rows = dims
    mem_rows = slots * TF
    scale = 1.0 / math.sqrt(HEAD_DIM)
    g = lax.axis_index("frame")
    z = lax.axis_index("head")

    barrier = pltpu.get_barrier_semaphore()
    offsets = sorted({(1 + i) % groups for i in range(slots)} | {(-1 - i) % groups for i in range(slots)})
    for off in offsets:
        pl.semaphore_signal(
            barrier, inc=1, device_id={"frame": lax.rem(g + off, groups)}, device_id_type=MESH
        )
    for off in range(1, zs):
        pl.semaphore_signal(
            barrier, inc=1, device_id={"head": lax.rem(z + off, zs)}, device_id_type=MESH
        )
    pl.semaphore_wait(barrier, len(offsets) + zs - 1)

    my_rows = pl.ds(pl.multiple_of(z * part, part), part)

    def landing(h, a, rows):
        if a < 2:
            return kv.at[h, a, rows]
        return qg.at[h, a - 2, rows]

    def send_inputs(h):
        for a, src in enumerate((k_in, v_in, q_in, g_in)):
            for off in range(zs - 1, 0, -1):
                peer = lax.rem(z + off, zs)
                cols = pl.ds(pl.multiple_of((peer * heads + h) * HEAD_DIM, HEAD_DIM), HEAD_DIM)
                pltpu.make_async_remote_copy(
                    src_ref=src.at[:, cols],
                    dst_ref=landing(h, a, my_rows),
                    send_sem=in_send.at[a],
                    recv_sem=in_recv.at[h, a],
                    device_id={"head": peer},
                    device_id_type=MESH,
                ).start()
            cols = pl.ds(pl.multiple_of((z * heads + h) * HEAD_DIM, HEAD_DIM), HEAD_DIM)
            pltpu.make_async_copy(
                src.at[:, cols], landing(h, a, my_rows), in_recv.at[h, a]
            ).start()

    def wait_for(ref, sem):
        pltpu.make_async_copy(ref, ref, sem).wait()

    def send_output(h, a):
        dst = (o_out, dq_out, dk_out, dv_out)[a]
        cols = pl.ds(pl.multiple_of((z * heads + h) * HEAD_DIM, HEAD_DIM), HEAD_DIM)
        for off in range(zs - 1, 0, -1):
            peer = lax.rem(z + off, zs)
            pltpu.make_async_remote_copy(
                src_ref=outs.at[h, a, pl.ds(pl.multiple_of(peer * part, part), part)],
                dst_ref=dst.at[:, cols],
                send_sem=out_send.at[a],
                recv_sem=out_recv.at[a],
                device_id={"head": peer},
                device_id_type=MESH,
            ).start()
        pltpu.make_async_copy(outs.at[h, a, my_rows], dst.at[:, cols], out_recv.at[a]).start()

    lax.fori_loop(0, min(AHEAD, heads), lambda h, c: (send_inputs(h), c)[1], 0)

    if key_rows > ROWS + mem_rows:
        rest = key_rows - ROWS - mem_rows

        def clear(h, c):
            kv[h, :, ROWS + mem_rows :, :] = jnp.zeros((2, rest, HEAD_DIM), jnp.bfloat16)
            return c

        lax.fori_loop(0, heads, clear, 0)

    def fetch(h):
        for a in range(2):
            wait_for(landing(h, a, pl.ds(0, ROWS)), in_recv.at[h, a])
        for a in range(2):
            mem_send[h, a] = jnp.dot(
                pick_ref[...], kv[h, a, :ROWS, :], preferred_element_type=jnp.float32
            ).astype(jnp.bfloat16)
        for i in range(slots):
            pltpu.make_async_remote_copy(
                src_ref=mem_send.at[h, :, pl.ds(i * TF, TF)],
                dst_ref=kv.at[h, :, pl.ds(ROWS + i * TF, TF)],
                send_sem=mem_ssem,
                recv_sem=mem_rsem.at[h],
                device_id={"frame": lax.rem(g + 1 + i, groups)},
                device_id_type=MESH,
            ).start()

    def attend(h):
        slot = lax.rem(h, 2)
        for a in range(2, 4):
            wait_for(landing(h, a, pl.ds(0, ROWS)), in_recv.at[h, a])
        wait_for(kv.at[h, :, pl.ds(ROWS, mem_rows)], mem_rsem.at[h])
        acc[slot] = jnp.zeros(acc.shape[1:], jnp.float32)

        def block(b, c):
            rows = pl.ds(pl.multiple_of(b * QBLOCK, QBLOCK), QBLOCK)
            query = qg[h, 0, rows, :]
            grad = qg[h, 1, rows, :]
            key = kv[h, 0]
            value = kv[h, 1]
            s = lax.dot_general(
                query, key, (((1,), (1,)), ((), ())), preferred_element_type=jnp.float32
            )
            s = s * (scale * math.log2(math.e)) + bias_ref[...]
            p = jnp.exp2(s - jnp.max(s, axis=1, keepdims=True))
            w = p * (1.0 / jnp.sum(p, axis=1, keepdims=True))
            wb = w.astype(jnp.bfloat16)
            outs[h, 0, rows, :] = jnp.dot(
                wb, value, preferred_element_type=jnp.float32
            ).astype(jnp.bfloat16)
            dp = lax.dot_general(
                grad, value, (((1,), (1,)), ((), ())), preferred_element_type=jnp.float32
            )
            delta = jnp.sum(w * dp, axis=1, keepdims=True)
            ds = (w * (dp - delta)).astype(jnp.bfloat16)
            outs[h, 1, rows, :] = (
                jnp.dot(ds, key, preferred_element_type=jnp.float32) * scale
            ).astype(jnp.bfloat16)
            acc[slot, 0] += lax.dot_general(
                ds, query, (((0,), (0,)), ((), ())), preferred_element_type=jnp.float32
            )
            acc[slot, 1] += lax.dot_general(
                wb, grad, (((0,), (0,)), ((), ())), preferred_element_type=jnp.float32
            )
            return c

        lax.fori_loop(0, ROWS // QBLOCK, block, 0)
        mem = pl.ds(ROWS, mem_rows)
        mem_grad[h, 0] = (acc[slot, 0, mem, :] * scale).astype(jnp.bfloat16)
        mem_grad[h, 1] = acc[slot, 1, mem, :].astype(jnp.bfloat16)
        for i in range(slots):
            pltpu.make_async_remote_copy(
                src_ref=mem_grad.at[h, :, pl.ds(i * TF, TF)],
                dst_ref=back.at[h, :, pl.ds(i * TF, TF)],
                send_sem=back_ssem,
                recv_sem=back_rsem.at[h],
                device_id={"frame": lax.rem(g + groups - 1 - i, groups)},
                device_id_type=MESH,
            ).start()
        send_output(h, 0)
        send_output(h, 1)

    def finish(h):
        slot = lax.rem(h, 2)
        wait_for(back.at[h], back_rsem.at[h])
        for a in range(2):
            extra = jnp.dot(spread_ref[...], back[h, a], preferred_element_type=jnp.float32)
            own = acc[slot, a, :ROWS, :]
            if a == 0:
                own = own * scale
            outs[h, 2 + a] = (own + extra).astype(jnp.bfloat16)
            send_output(h, 2 + a)

    def step(t, c):
        @pl.when(t < heads - AHEAD)
        def _():
            send_inputs(t + AHEAD)

        @pl.when(t < heads)
        def _():
            fetch(t)

        @pl.when(t >= 2)
        def _():
            finish(t - 2)

        @pl.when(jnp.logical_and(t >= 1, t <= heads))
        def _():
            attend(t - 1)

        return c

    lax.fori_loop(0, heads + 2, step, 0)

    sent = pl.ds(0, (zs - 1) * heads * HEAD_DIM)
    for a, src in enumerate((k_in, v_in, q_in, g_in)):
        wait_for(src.at[:, sent], in_send.at[a])
    wait_for(mem_send, mem_ssem)
    wait_for(mem_grad, back_ssem)
    for a, dst in enumerate((o_out, dq_out, dk_out, dv_out)):
        wait_for(outs.at[:, a, pl.ds(0, (zs - 1) * part)], out_send.at[a])
        wait_for(dst, out_recv.at[a])


def local(queries, keys, values, out_grad, memory_frames, frame_tokens):
    groups = lax.axis_size("frame")
    zs = lax.axis_size("head")
    part, feat = queries.shape
    heads = feat // HEAD_DIM // zs
    slots = memory_frames.shape[1]
    mem_rows = slots * TF
    key_rows = -(-(ROWS + mem_rows) // 128) * 128
    g = lax.axis_index("frame")
    slot_ids = jnp.arange(slots, dtype=jnp.int32)

    mine = lax.dynamic_index_in_dim(memory_frames, g, 0, keepdims=False)
    all_frames = jnp.arange(frame_tokens.shape[0], dtype=jnp.int32)
    mem_counts = jnp.sum(
        jnp.where(mine[:, None] == all_frames[None, :], frame_tokens[None, :], 0), axis=1
    )
    own_counts = lax.dynamic_slice_in_dim(frame_tokens, g * FRAMES_DEV, FRAMES_DEV)
    counts = jnp.concatenate(
        [own_counts, mem_counts, jnp.zeros((key_rows // TF - FRAMES_DEV - slots,), jnp.int32)]
    )
    live = jnp.arange(TF, dtype=jnp.int32)[None, :] < counts[:, None]
    bias = jnp.where(live, 0.0, -jnp.inf).astype(jnp.float32).reshape(1, key_rows)

    askers = (g + 1 + slot_ids) % groups
    hit = jnp.arange(groups, dtype=jnp.int32)[:, None] == askers[None, :]
    wanted = jnp.sum(jnp.where(hit, memory_frames, 0), axis=0) % FRAMES_DEV
    mem_at = (wanted[:, None] * TF + jnp.arange(TF, dtype=jnp.int32)[None, :]).reshape(mem_rows)
    row_ids = jnp.arange(ROWS, dtype=jnp.int32)
    pick = (mem_at[:, None] == row_ids[None, :]).astype(jnp.bfloat16)
    spread = (row_ids[:, None] == mem_at[None, :]).astype(jnp.bfloat16)

    dims = (groups, zs, heads, slots, part, key_rows)
    any_spec = pl.BlockSpec(memory_space=pl.ANY)
    vmem_spec = pl.BlockSpec(memory_space=pltpu.VMEM)
    bf16 = jnp.bfloat16
    pairs = heads * ROWS * key_rows
    return pl.pallas_call(
        functools.partial(attention_kernel, dims),
        out_shape=[jax.ShapeDtypeStruct((part, feat), bf16)] * 4,
        in_specs=[any_spec] * 4 + [vmem_spec] * 3,
        out_specs=[any_spec] * 4,
        scratch_shapes=[
            pltpu.VMEM((heads, 2, ROWS, HEAD_DIM), bf16),
            pltpu.VMEM((heads, 2, key_rows, HEAD_DIM), bf16),
            pltpu.VMEM((heads, 2, mem_rows, HEAD_DIM), bf16),
            pltpu.VMEM((heads, 2, mem_rows, HEAD_DIM), bf16),
            pltpu.VMEM((heads, 2, mem_rows, HEAD_DIM), bf16),
            pltpu.VMEM((heads, 4, ROWS, HEAD_DIM), bf16),
            pltpu.VMEM((2, 2, key_rows, HEAD_DIM), jnp.float32),
            pltpu.SemaphoreType.DMA((4,)),
            pltpu.SemaphoreType.DMA((heads, 4)),
            pltpu.SemaphoreType.DMA,
            pltpu.SemaphoreType.DMA((heads,)),
            pltpu.SemaphoreType.DMA,
            pltpu.SemaphoreType.DMA((heads,)),
            pltpu.SemaphoreType.DMA((4,)),
            pltpu.SemaphoreType.DMA((4,)),
        ],
        compiler_params=pltpu.CompilerParams(
            collective_id=0, has_side_effects=True, vmem_limit_bytes=60 * 1024 * 1024
        ),
        cost_estimate=pl.CostEstimate(
            flops=10 * pairs * HEAD_DIM, bytes_accessed=16 * part * feat, transcendentals=pairs
        ),
    )(queries, keys, values, out_grad, bias, pick, spread)


def solution(mesh):
    rows = P(("frame", "head"), None)
    return jax.shard_map(
        local,
        mesh=mesh,
        in_specs=(rows, rows, rows, rows, P(), P()),
        out_specs=(rows, rows, rows, rows),
        check_vma=False,
    )
```

time: 902 us -> 477 us (0.53)
  Pallas kernels: 0 us -> 460 us
  waiting for transfers between devices: 424 us -> 0 us
  matrix products: 242 us -> 0 us
  local copies, waits for them, and re-layouts: 96.2 us -> 12.6 us
  other arithmetic: 75.6 us -> 4.31 us
  starting transfers between devices: 53.9 us -> 0 us
    pallas_call x0 -> x1, Pallas kernels: none -> 460 us  [local(): pl.pallas_call(functools.partial(attention_kernel, dims), out_shape=[jax....]
    all_to_all x12 -> x0, waiting for transfers between devices: 424 us -> none  [the longest x1 55.1 us: local(): lax.all_to_all(values, 'head', split_axis=1, concat_axis=0, tiled=True)]
    dot_general x64 -> x0, matrix products: 242 us -> none  [the longest x10 79.3 us: attend(): jnp.einsum('rd,kd->rk', grad_rows, member[1], preferred_element_type=jnp....]
    all_to_all x12 -> x0, starting transfers between devices: 53.9 us -> none  [the longest x1 6.32 us: local(): lax.all_to_all(values, 'head', split_axis=1, concat_axis=0, tiled=True)]
    convert_element_type x5 -> x2, other arithmetic: 53.4 us -> 2.53 us  [the longest x1 1.39 us: local(): spread = (row_ids[:, None] == mem_at[None, :]).astype(jnp.bfloat16)]
    all_to_all x8 -> x0, local copies, waits for them, and re-layouts: 28.6 us -> none  [the longest x1 4.57 us: local(): lax.all_to_all(out_grad, 'head', split_axis=1, concat_axis=0, tiled=True)]
    unnamed x166 -> x10, local copies, waits for them, and re-layouts: 32 us -> 10.4 us
    reduce_sum x3 -> x2, other arithmetic: 18.5 us -> 1.54 us  [the longest x1 0.84 us: local(): jnp.sum(jnp.where(mine[:, None] == all_frames[None, :], frame_tokens[None...]
  transfers between devices with their start and end apart: 12 -> 0, of which waited for: 11 -> 0; matrix products, arithmetic and copies ran while one was open for 16% -> 0% of each run, Pallas kernels for 0% -> 0%
where the time goes in v1:
time: 477 us
  Pallas kernels  460 us (96%)
  local copies, waits for them, and re-layouts  12.6 us (3%)
    pallas_call x1, Pallas kernels, local(): pl.pallas_call(functools.partial(attention_kernel, dims), out_shape=[jax....  460 us
    unnamed x10, local copies, waits for them, and re-layouts  10.4 us

profile of v1, /device:TPU:0, one launch (start us, length us, event | category | flops | bytes accessed | tf_op | source)
XLA Modules:
  0.0 477.1 jit_solution(1352167364008185841)
XLA Ops:
  0.6 0.7 dynamic-slice_bitcast_fusion
  1.3 0.8 select_reduce_fusion.1
  2.2 0.7 dynamic_slice.7
  2.9 0.1 pad_add_fusion
  3.0 0.7 select_reduce_fusion
  3.7 0.1 iota_add_fusion
  3.8 0.1 add.72
  3.9 0.1 fusion.2
  3.9 0.7 select_n.52.bias_ref
  4.6 1.1 fusion.1.pick_ref
  5.7 1.4 fusion.spread_ref
  7.1 459.5 %shard_map.93 = (bf16[256,5120]{1,0:T(8,128)(2,1)}, bf16[256,5120]{1,0:T(8,128)(2,1)}, bf16[256,5120]{1,0:T(8,128)(2,1)}, bf16[256,5120]{1,0:T(8,128)(2,1)}) custom-call(bf16[256,5120]{1,0:T(8,128)(2,1)} %q_in.1, bf16[256,5120]{1,0:T(8,128)(2,1)} %k_in.1, bf16[256,5120]{1,0:T(8,128)(2,1)} %v_in.1, bf16[256,5120]{1,0:T(8,128)(2,1)} %g_in.1, ...), custom_call_target="tpu_custom_call" | custom-call | flops 20132659200 | bytes 20971520 | tf_op jit(solution)/shard_map/pallas_call | solution.py:249
  466.7 0.0 copy-start.2
  466.7 3.6 copy.14
  470.2 0.0 copy-done.2
  470.2 0.0 copy-start.1
  470.2 1.5 copy.15
  471.7 1.2 copy-done.1
  472.9 0.0 copy-start
  472.9 1.5 copy.16
  474.4 1.2 copy-done
  475.6 1.5 copy.17
  (2 shorter events, 0.0 us)
Async XLA Ops:
  466.7 3.6 copy-start.2
  470.2 2.7 copy-start.1
  472.9 2.7 copy-start

commit v2 on v1

--- a/solution.py
+++ b/solution.py
@@ -19,9 +19,9 @@
 
 def attention_kernel(
     dims,
-    q_in, k_in, v_in, g_in, bias_ref, pick_ref, spread_ref,
+    q_in, k_in, v_in, g_in, frames_ref, tokens_ref,
     o_out, dq_out, dk_out, dv_out,
-    qg, kv, mem_send, mem_grad, back, outs, acc,
+    bias_ref, pick_ref, spread_ref, qg, kv, mem_send, mem_grad, back, outs, acc,
     in_send, in_recv, mem_ssem, mem_rsem, back_ssem, back_rsem, out_send, out_recv,
 ):
     groups, zs, heads, slots, part, key_rows = dims
@@ -51,7 +51,7 @@
 
     def send_inputs(h):
         for a, src in enumerate((k_in, v_in, q_in, g_in)):
-            for off in range(zs - 1, 0, -1):
+            for off in range(1, zs):
                 peer = lax.rem(z + off, zs)
                 cols = pl.ds(pl.multiple_of((peer * heads + h) * HEAD_DIM, HEAD_DIM), HEAD_DIM)
                 pltpu.make_async_remote_copy(
@@ -73,7 +73,7 @@
     def send_output(h, a):
         dst = (o_out, dq_out, dk_out, dv_out)[a]
         cols = pl.ds(pl.multiple_of((z * heads + h) * HEAD_DIM, HEAD_DIM), HEAD_DIM)
-        for off in range(zs - 1, 0, -1):
+        for off in range(1, zs):
             peer = lax.rem(z + off, zs)
             pltpu.make_async_remote_copy(
                 src_ref=outs.at[h, a, pl.ds(pl.multiple_of(peer * part, part), part)],
@@ -86,6 +86,29 @@
         pltpu.make_async_copy(outs.at[h, a, my_rows], dst.at[:, cols], out_recv.at[a]).start()
 
     lax.fori_loop(0, min(AHEAD, heads), lambda h, c: (send_inputs(h), c)[1], 0)
+
+    wanted = [
+        lax.rem(frames_ref[lax.rem(g + 1 + i, groups), i], FRAMES_DEV) * TF for i in range(slots)
+    ]
+    counts = [tokens_ref[g * FRAMES_DEV + f] for f in range(FRAMES_DEV)]
+    counts += [tokens_ref[frames_ref[g, i]] for i in range(slots)]
+
+    def chosen(shape, dim, entries):
+        place = lax.broadcasted_iota(jnp.int32, shape, dim)
+        segment = place // TF
+        picked = jnp.zeros(shape, jnp.int32)
+        for number, entry in enumerate(entries):
+            picked = jnp.where(segment == number, entry, picked)
+        return place - segment * TF, picked
+
+    place, count = chosen((1, key_rows), 1, counts)
+    bias_ref[...] = jnp.where(place < count, 0.0, -jnp.inf).astype(jnp.float32)
+    place, start = chosen((mem_rows, 1), 0, wanted)
+    columns = lax.broadcasted_iota(jnp.int32, (mem_rows, ROWS), 1)
+    pick_ref[...] = jnp.where(columns == place + start, 1.0, 0.0).astype(jnp.bfloat16)
+    place, start = chosen((1, mem_rows), 1, wanted)
+    row_ids = lax.broadcasted_iota(jnp.int32, (ROWS, mem_rows), 0)
+    spread_ref[...] = jnp.where(row_ids == place + start, 1.0, 0.0).astype(jnp.bfloat16)
 
     if key_rows > ROWS + mem_rows:
         rest = key_rows - ROWS - mem_rows
@@ -218,40 +241,20 @@
     slots = memory_frames.shape[1]
     mem_rows = slots * TF
     key_rows = -(-(ROWS + mem_rows) // 128) * 128
-    g = lax.axis_index("frame")
-    slot_ids = jnp.arange(slots, dtype=jnp.int32)
-
-    mine = lax.dynamic_index_in_dim(memory_frames, g, 0, keepdims=False)
-    all_frames = jnp.arange(frame_tokens.shape[0], dtype=jnp.int32)
-    mem_counts = jnp.sum(
-        jnp.where(mine[:, None] == all_frames[None, :], frame_tokens[None, :], 0), axis=1
-    )
-    own_counts = lax.dynamic_slice_in_dim(frame_tokens, g * FRAMES_DEV, FRAMES_DEV)
-    counts = jnp.concatenate(
-        [own_counts, mem_counts, jnp.zeros((key_rows // TF - FRAMES_DEV - slots,), jnp.int32)]
-    )
-    live = jnp.arange(TF, dtype=jnp.int32)[None, :] < counts[:, None]
-    bias = jnp.where(live, 0.0, -jnp.inf).astype(jnp.float32).reshape(1, key_rows)
-
-    askers = (g + 1 + slot_ids) % groups
-    hit = jnp.arange(groups, dtype=jnp.int32)[:, None] == askers[None, :]
-    wanted = jnp.sum(jnp.where(hit, memory_frames, 0), axis=0) % FRAMES_DEV
-    mem_at = (wanted[:, None] * TF + jnp.arange(TF, dtype=jnp.int32)[None, :]).reshape(mem_rows)
-    row_ids = jnp.arange(ROWS, dtype=jnp.int32)
-    pick = (mem_at[:, None] == row_ids[None, :]).astype(jnp.bfloat16)
-    spread = (row_ids[:, None] == mem_at[None, :]).astype(jnp.bfloat16)
-
     dims = (groups, zs, heads, slots, part, key_rows)
     any_spec = pl.BlockSpec(memory_space=pl.ANY)
-    vmem_spec = pl.BlockSpec(memory_space=pltpu.VMEM)
+    smem_spec = pl.BlockSpec(memory_space=pltpu.SMEM)
     bf16 = jnp.bfloat16
     pairs = heads * ROWS * key_rows
     return pl.pallas_call(
         functools.partial(attention_kernel, dims),
         out_shape=[jax.ShapeDtypeStruct((part, feat), bf16)] * 4,
-        in_specs=[any_spec] * 4 + [vmem_spec] * 3,
+        in_specs=[any_spec] * 4 + [smem_spec] * 2,
         out_specs=[any_spec] * 4,
         scratch_shapes=[
+            pltpu.VMEM((1, key_rows), jnp.float32),
+            pltpu.VMEM((mem_rows, ROWS), bf16),
+            pltpu.VMEM((ROWS, mem_rows), bf16),
             pltpu.VMEM((heads, 2, ROWS, HEAD_DIM), bf16),
             pltpu.VMEM((heads, 2, key_rows, HEAD_DIM), bf16),
             pltpu.VMEM((heads, 2, mem_rows, HEAD_DIM), bf16),
@@ -274,7 +277,7 @@
         cost_estimate=pl.CostEstimate(
             flops=10 * pairs * HEAD_DIM, bytes_accessed=16 * part * feat, transcendentals=pairs
         ),
-    )(queries, keys, values, out_grad, bias, pick, spread)
+    )(queries, keys, values, out_grad, memory_frames, frame_tokens)
 
 
 def solution(mesh):

time: 477 us -> 469 us (0.983)
  no operation moved by 1% of the time
where the time goes in v2:
time: 469 us
  Pallas kernels  458 us (98%)
  local copies, waits for them, and re-layouts  10.4 us (2%)
    pallas_call x1, Pallas kernels, local(): pl.pallas_call(functools.partial(attention_kernel, dims), out_shape=[jax....  458 us
    unnamed x10, local copies, waits for them, and re-layouts  10.4 us

profile of v2, /device:TPU:0, one launch (start us, length us, event | category | flops | bytes accessed | tf_op | source)
XLA Modules:
  0.0 468.9 jit_solution(10721817788730251935)
XLA Ops:
  0.6 457.9 %shard_map.93 = (bf16[256,5120]{1,0:T(8,128)(2,1)}, bf16[256,5120]{1,0:T(8,128)(2,1)}, bf16[256,5120]{1,0:T(8,128)(2,1)}, bf16[256,5120]{1,0:T(8,128)(2,1)}) custom-call(bf16[256,5120]{1,0:T(8,128)(2,1)} %q_in.1, bf16[256,5120]{1,0:T(8,128)(2,1)} %k_in.1, bf16[256,5120]{1,0:T(8,128)(2,1)} %v_in.1, bf16[256,5120]{1,0:T(8,128)(2,1)} %g_in.1, ...), custom_call_target="tpu_custom_call" | custom-call | flops 20132659200 | bytes 20971520 | tf_op jit(solution)/shard_map/pallas_call | solution.py:249
  458.5 0.0 copy-start.2
  458.5 3.6 copy.14
  462.1 0.0 copy-done.2
  462.1 0.0 copy-start.1
  462.1 1.5 copy.15
  463.6 1.2 copy-done.1
  464.8 0.0 copy-start
  464.8 1.5 copy.16
  466.3 1.2 copy-done
  467.5 1.5 copy.17
Async XLA Ops:
  458.5 3.6 copy-start.2
  462.1 2.7 copy-start.1
  464.8 2.7 copy-start
